TPU v7x, 32 devices: a whole 2x2x4 slice. The times are simulated.
32 devices in a mesh: dom: 8 (over z, y), sub: 4 (over x, core).
Axes of the slice: x: 2, y: 2, z: 4, core: 2. Of those that a mesh axis runs over, the one named last changes fastest.
Arguments:
- rhs: float32 [6, 16384], P(None, ('dom', 'sub')), may hold values from -6 to 6
- precond: float32 [6, 6, 16384], P(None, None, ('dom', 'sub'))
- diag_blocks: float32 [6, 6, 16384], P(None, None, ('dom', 'sub'))
- off_blocks: float32 [6, 6, 6, 16384], P(None, None, None, ('dom', 'sub')), may hold values from -0.5 to 0.5
- neighbours: int32 [6, 16384], P(None, ('dom', 'sub')), may hold values from 0 to 1023
- colours: int32 [16384], P(('dom', 'sub')), may hold values from 0 to 3, as said below
- send_lists: int32 [4, 4, 1024], P(None, None, ('dom', 'sub')), may hold values from 0 to 511, as said below
Outputs:
- correction: float32 [6, 16384], P(None, ('dom', 'sub'))
- new_residual: float32 [6, 16384], P(None, ('dom', 'sub'))
Inputs may be any that keep to these rules, and one draw needn't show every extreme that they name: colours[n] equals c exactly for the nodes listed under colour c in its device's send_lists; each colour holds 128 nodes of every device. `send_lists`: on each device the 512 entries are the 512 local nodes, each once; entry [d, c, h] is a node of colour c.
All inputs are finite; a program needn't handle non-finite values.
Results may differ from a plain program's by a relative error of at most 0.0001.
Values sent between devices are 32-bit elements; how exact they have to be, the bound alone decides.
A program may use at most 64 MiB of HBM per device.

v0:
```python
import jax
import jax.numpy as jnp
from jax import lax
from jax.sharding import PartitionSpec as P


def from_behind(block, axis, distance):
    devices = range(lax.axis_size(axis))
    route = [((i - distance) % len(devices), i) for i in devices]
    return lax.ppermute(block, axis, route)


def neighbour_sum(extended, neighbours, off_blocks):
    gathered = jnp.take(extended, neighbours, axis=1)
    return jnp.einsum("kabn,bkn->an", off_blocks, gathered, precision=lax.Precision.HIGHEST)


def apply_block(blocks, field):
    return jnp.einsum("abn,bn->an", blocks, field, precision=lax.Precision.HIGHEST)


def trade(outgoing):
    from_lower_dom = from_behind(outgoing[:, 0], "dom", 1)
    from_upper_dom = from_behind(outgoing[:, 1], "dom", -1)
    from_lower_sub = from_behind(outgoing[:, 2], "sub", 1)
    from_upper_sub = from_behind(outgoing[:, 3], "sub", -1)
    return jnp.stack([from_lower_dom, from_upper_dom, from_lower_sub, from_upper_sub], axis=1)


def shards(rhs, precond, diag_blocks, off_blocks, neighbours, colours, send_lists):
    width = rhs.shape[0]
    nodes_dev = rhs.shape[1]
    slots = send_lists.shape[2]
    correction = jnp.zeros((width, nodes_dev), jnp.float32)
    halo_buffer = jnp.zeros((width, 4, 4, slots), jnp.float32)
    for colour in range(4):
        extended = jnp.concatenate([correction, halo_buffer.reshape(width, 16 * slots)], axis=1)
        coupled = neighbour_sum(extended, neighbours, off_blocks)
        candidate = apply_block(precond, rhs - coupled)
        correction = jnp.where((colours == colour)[None, :], candidate, correction)
        halo_buffer = trade(correction[:, send_lists])
    extended = jnp.concatenate([correction, halo_buffer.reshape(width, 16 * slots)], axis=1)
    coupled = neighbour_sum(extended, neighbours, off_blocks)
    new_residual = rhs - apply_block(diag_blocks, correction) - coupled
    return (correction, new_residual)


def solution(mesh):
    placed = (
        P(None, ("dom", "sub")),
        P(None, None, ("dom", "sub")),
        P(None, None, ("dom", "sub")),
        P(None, None, None, ("dom", "sub")),
        P(None, ("dom", "sub")),
        P(("dom", "sub")),
        P(None, None, ("dom", "sub")),
    )
    return jax.shard_map(
        shards,
        mesh=mesh,
        in_specs=placed,
        out_specs=(P(None, ("dom", "sub")), P(None, ("dom", "sub"))),
        check_vma=False,
    )
```

profile of v0, /device:TPU:0, one launch (start us, length us, event | category | flops | bytes accessed | tf_op | source)
XLA Modules:
  0.0 111.0 jit_solution(6162885994956023522)
XLA Ops:
  0.6 0.7 compare_and_fusion
  1.4 0.7 compare_select_fusion
  2.1 0.7 broadcast_compare_fusion.3
  2.8 0.7 compare_select_fusion.1
  3.6 10.8 %gather_fusion.4 = f32[3072,6]{1,0:T(8,128)} fusion(f32[6,1024]{0,1:T(8,128)S(1)} %concatenate.15, s32[3072]{0:T(1024)S(1)} %broadcast_clamp_fusion), kind=kCustom, calls=%fused_computation.clone | custom fusion | bytes 159744 | tf_op jit(solution)/shard_map/jit(_take)/gather | solution.py:14
  14.5 1.7 %select_bitcast_fusion.4 = f32[512,6,6]{1,0,2:T(8,128)S(1)} fusion(f32[6,512,6]{2,1,0:T(8,128)} %bitcast.152, pred[6,512]{1,0:T(8,128)(4,1)S(1)} %compare_and_fusion), kind=kLoop, calls=%fused_computation.13 | loop fusion | flops 18432 | bytes 150528
  16.2 0.5 copy.127
  16.7 0.6 copy-done
  17.7 1.0 gather_fusion
  18.8 3.0 %collective-permute-start = (f32[6,4,32]{0,2,1:T(8,128)S(1)}, f32[6,4,32]{0,2,1:T(8,128)S(1)}, u32[]{:S(2)}, u32[]{:S(2)}) collective-permute-start(f32[6,4,32]{0,2,1:T(8,128)S(1)} %get-tuple-element.23), channel_id=1, source_target_pairs={{28,0},{0,4},{4,8},{8,12},{12,16},{16,20},{20,24},{24,28},{29,1},{... | collective-permute-start | bytes 9224 | tf_op jit(solution)/shard_map/ppermute | solution.py:10
  21.8 3.2 %collective-permute-start.1 = (f32[6,4,32]{0,2,1:T(8,128)S(1)}, f32[6,4,32]{0,2,1:T(8,128)S(1)}, u32[]{:S(2)}, u32[]{:S(2)}) collective-permute-start(f32[6,4,32]{0,2,1:T(8,128)S(1)} %get-tuple-element.25), channel_id=1, source_target_pairs={{4,0},{8,4},{12,8},{16,12},{20,16},{24,20},{28,24},{0,28},{5,1},{9... | collective-permute-start | bytes 9224 | tf_op jit(solution)/shard_map/ppermute | solution.py:10
  25.0 1.4 %collective-permute-start.3 = (f32[6,4,32]{0,2,1:T(8,128)S(1)}, f32[6,4,32]{0,2,1:T(8,128)S(1)}, u32[]{:S(2)}, u32[]{:S(2)}) collective-permute-start(f32[6,4,32]{0,2,1:T(8,128)S(1)} %get-tuple-element.26), channel_id=1, source_target_pairs={{1,0},{2,1},{3,2},{0,3},{5,4},{6,5},{7,6},{4,7},{9,8},{10,9},{11,1... | collective-permute-start | bytes 9224 | tf_op jit(solution)/shard_map/ppermute | solution.py:10
  26.4 0.8 collective-permute-done
  27.2 0.8 collective-permute-done.1
  27.9 0.4 collective-permute-done.3
  28.4 10.8 %gather_fusion.5 = f32[3072,6]{1,0:T(8,128)} fusion(f32[6,1024]{0,1:T(8,128)S(1)} %pad_maximum_fusion, s32[3072]{0:T(1024)S(1)} %broadcast_clamp_fusion), kind=kCustom, calls=%fused_computation.1.clone | custom fusion | bytes 159744 | tf_op jit(solution)/shard_map/jit(_take)/gather | solution.py:14
  39.2 1.7 %select_bitcast_fusion.3 = f32[512,6,6]{1,0,2:T(8,128)S(1)} fusion(f32[6,512,6]{2,1,0:T(8,128)} %bitcast.153, pred[6,512]{1,0:T(8,128)(4,1)S(1)} %compare_and_fusion), kind=kLoop, calls=%fused_computation.12 | loop fusion | flops 18432 | bytes 150528
  40.9 0.5 copy.129
  41.9 1.0 gather_fusion.1
  43.0 0.4 collective-permute-start.4
  43.4 1.5 %collective-permute-start.6 = (f32[6,4,32]{0,2,1:T(8,128)S(1)}, f32[6,4,32]{0,2,1:T(8,128)S(1)}, u32[]{:S(2)}, u32[]{:S(2)}) collective-permute-start(f32[6,4,32]{0,2,1:T(8,128)S(1)} %get-tuple-element.20), channel_id=1, source_target_pairs={{3,0},{0,1},{1,2},{2,3},{7,4},{4,5},{5,6},{6,7},{11,8},{8,9},{9,10... | collective-permute-start | bytes 9224 | tf_op jit(solution)/shard_map/ppermute | solution.py:10
  44.8 4.4 %collective-permute-start.5 = (f32[6,4,32]{0,2,1:T(8,128)S(1)}, f32[6,4,32]{0,2,1:T(8,128)S(1)}, u32[]{:S(2)}, u32[]{:S(2)}) collective-permute-start(f32[6,4,32]{0,2,1:T(8,128)S(1)} %get-tuple-element.21), channel_id=1, source_target_pairs={{4,0},{8,4},{12,8},{16,12},{20,16},{24,20},{28,24},{0,28},{5,1},{9... | collective-permute-start | bytes 9224 | tf_op jit(solution)/shard_map/ppermute | solution.py:10
  49.2 0.8 collective-permute-done.4
  50.0 1.1 %collective-permute-done.5 = f32[6,4,32]{0,2,1:T(8,128)S(1)} collective-permute-done((f32[6,4,32]{0,2,1:T(8,128)S(1)}, f32[6,4,32]{0,2,1:T(8,128)S(1)}, u32[]{:S(2)}, u32[]{:S(2)}) %collective-permute-start.5) | collective-permute-done | bytes 3104 | tf_op jit(solution)/shard_map/ppermute | solution.py:10
  51.2 10.8 %gather_fusion.6 = f32[3072,6]{1,0:T(8,128)} fusion(f32[6,1024]{0,1:T(8,128)S(1)} %pad_maximum_fusion.1, s32[3072]{0:T(1024)S(1)} %broadcast_clamp_fusion), kind=kCustom, calls=%fused_computation.2.clone | custom fusion | bytes 159744 | tf_op jit(solution)/shard_map/jit(_take)/gather | solution.py:14
  62.0 1.7 %select_bitcast_fusion.2 = f32[512,6,6]{1,0,2:T(8,128)S(1)} fusion(f32[6,512,6]{2,1,0:T(8,128)} %bitcast.154, pred[6,512]{1,0:T(8,128)(4,1)S(1)} %compare_and_fusion), kind=kLoop, calls=%fused_computation.11 | loop fusion | flops 18432 | bytes 150528
  63.8 0.5 copy.131
  64.7 1.0 gather_fusion.2
  65.9 1.8 %collective-permute-start.10 = (f32[6,4,32]{0,2,1:T(8,128)S(1)}, f32[6,4,32]{0,2,1:T(8,128)S(1)}, u32[]{:S(2)}, u32[]{:S(2)}) collective-permute-start(f32[6,4,32]{0,2,1:T(8,128)S(1)} %get-tuple-element.16), channel_id=1, source_target_pairs={{3,0},{0,1},{1,2},{2,3},{7,4},{4,5},{5,6},{6,7},{11,8},{8,9},{9,10... | collective-permute-start | bytes 9224 | tf_op jit(solution)/shard_map/ppermute | solution.py:10
  67.6 4.4 %collective-permute-start.9 = (f32[6,4,32]{0,2,1:T(8,128)S(1)}, f32[6,4,32]{0,2,1:T(8,128)S(1)}, u32[]{:S(2)}, u32[]{:S(2)}) collective-permute-start(f32[6,4,32]{0,2,1:T(8,128)S(1)} %get-tuple-element.17), channel_id=1, source_target_pairs={{4,0},{8,4},{12,8},{16,12},{20,16},{24,20},{28,24},{0,28},{5,1},{9... | collective-permute-start | bytes 9224 | tf_op jit(solution)/shard_map/ppermute | solution.py:10
  72.0 0.4 collective-permute-start.11
  72.4 1.1 collective-permute-done.8
  73.5 0.4 collective-permute-done.9
  73.9 0.4 collective-permute-done.11
  74.4 10.8 %gather_fusion.7 = f32[3072,6]{1,0:T(8,128)} fusion(f32[6,1024]{0,1:T(8,128)S(1)} %pad_maximum_fusion.2, s32[3072]{0:T(1024)S(1)} %broadcast_clamp_fusion), kind=kCustom, calls=%fused_computation.3.clone | custom fusion | bytes 159744 | tf_op jit(solution)/shard_map/jit(_take)/gather | solution.py:14
  85.2 1.7 %select_bitcast_fusion.1 = f32[512,6,6]{1,0,2:T(8,128)S(1)} fusion(f32[6,512,6]{2,1,0:T(8,128)} %bitcast.155, pred[6,512]{1,0:T(8,128)(4,1)S(1)} %compare_and_fusion), kind=kLoop, calls=%fused_computation.10 | loop fusion | flops 18432 | bytes 150528
  86.9 0.5 copy.133
  87.9 1.0 gather_fusion.3
  89.1 1.4 %collective-permute-start.14 = (f32[6,4,32]{0,2,1:T(8,128)S(1)}, f32[6,4,32]{0,2,1:T(8,128)S(1)}, u32[]{:S(2)}, u32[]{:S(2)}) collective-permute-start(f32[6,4,32]{0,2,1:T(8,128)S(1)} %get-tuple-element.12), channel_id=1, source_target_pairs={{3,0},{0,1},{1,2},{2,3},{7,4},{4,5},{5,6},{6,7},{11,8},{8,9},{9,10... | collective-permute-start | bytes 9224 | tf_op jit(solution)/shard_map/ppermute | solution.py:10
  90.5 4.4 %collective-permute-start.13 = (f32[6,4,32]{0,2,1:T(8,128)S(1)}, f32[6,4,32]{0,2,1:T(8,128)S(1)}, u32[]{:S(2)}, u32[]{:S(2)}) collective-permute-start(f32[6,4,32]{0,2,1:T(8,128)S(1)} %get-tuple-element.13), channel_id=1, source_target_pairs={{4,0},{8,4},{12,8},{16,12},{20,16},{24,20},{28,24},{0,28},{5,1},{9... | collective-permute-start | bytes 9224 | tf_op jit(solution)/shard_map/ppermute | solution.py:10
  94.9 0.4 collective-permute-start.15
  95.4 0.7 copy.56
  96.1 0.4 collective-permute-done.12
  96.8 0.4 collective-permute-done.15
  97.3 10.8 %gather_fusion.8 = f32[3072,6]{1,0:T(8,128)} fusion(f32[6,1024]{0,1:T(8,128)S(1)} %pad_maximum_fusion.3, s32[3072]{0:T(1024)S(1)} %broadcast_clamp_fusion), kind=kCustom, calls=%fused_computation.4.clone | custom fusion | bytes 159744 | tf_op jit(solution)/shard_map/jit(_take)/gather | solution.py:14
  108.1 1.7 %select_bitcast_fusion = f32[512,6,6]{1,0,2:T(8,128)S(1)} fusion(f32[6,512,6]{2,1,0:T(8,128)} %bitcast.151, pred[6,512]{1,0:T(8,128)(4,1)S(1)} %compare_and_fusion), kind=kLoop, calls=%fused_computation.9 | loop fusion | flops 18432 | bytes 150528
  109.8 0.5 copy.136
  110.4 0.6 bitcast_subtract_fusion
  (57 shorter events, 3.0 us)
Async XLA Ops:
  16.2 1.1 copy-start
  16.2 1.2 %copy-start.2 = (f32[6,512]{1,0:T(8,128)S(1)}, f32[6,512]{1,0:T(8,128)}, u32[]{:S(2)}) copy-start(f32[6,512]{1,0:T(8,128)} %param.9) | copy-start | bytes 36868
  16.2 1.2 %copy-start.1 = (f32[6,6,512]{2,1,0:T(8,128)S(1)}, f32[6,6,512]{2,1,0:T(8,128)}, u32[]{:S(2)}) copy-start(f32[6,6,512]{2,1,0:T(8,128)} %param.10) | copy-start | bytes 221188
  18.8 8.4 %collective-permute-start = (f32[6,4,32]{0,2,1:T(8,128)S(1)}, f32[6,4,32]{0,2,1:T(8,128)S(1)}, u32[]{:S(2)}, u32[]{:S(2)}) collective-permute-start(f32[6,4,32]{0,2,1:T(8,128)S(1)} %get-tuple-element.23), channel_id=1, source_target_pairs={{28,0},{0,4},{4,8},{8,12},{12,16},{16,20},{20,24},{24,28},{29,1},{... | collective-permute-start | bytes 9224 | tf_op jit(solution)/shard_map/ppermute | solution.py:10
  21.8 5.3 %collective-permute-start.2 = (f32[6,4,32]{0,2,1:T(8,128)S(1)}, f32[6,4,32]{0,2,1:T(8,128)S(1)}, u32[]{:S(2)}, u32[]{:S(2)}) collective-permute-start(f32[6,4,32]{0,2,1:T(8,128)S(1)} %get-tuple-element.24), channel_id=1, source_target_pairs={{3,0},{0,1},{1,2},{2,3},{7,4},{4,5},{5,6},{6,7},{11,8},{8,9},{9,10... | collective-permute-start | bytes 9224 | tf_op jit(solution)/shard_map/ppermute | solution.py:10
  21.8 6.1 %collective-permute-start.1 = (f32[6,4,32]{0,2,1:T(8,128)S(1)}, f32[6,4,32]{0,2,1:T(8,128)S(1)}, u32[]{:S(2)}, u32[]{:S(2)}) collective-permute-start(f32[6,4,32]{0,2,1:T(8,128)S(1)} %get-tuple-element.25), channel_id=1, source_target_pairs={{4,0},{8,4},{12,8},{16,12},{20,16},{24,20},{28,24},{0,28},{5,1},{9... | collective-permute-start | bytes 9224 | tf_op jit(solution)/shard_map/ppermute | solution.py:10
  25.0 3.3 %collective-permute-start.3 = (f32[6,4,32]{0,2,1:T(8,128)S(1)}, f32[6,4,32]{0,2,1:T(8,128)S(1)}, u32[]{:S(2)}, u32[]{:S(2)}) collective-permute-start(f32[6,4,32]{0,2,1:T(8,128)S(1)} %get-tuple-element.26), channel_id=1, source_target_pairs={{1,0},{2,1},{3,2},{0,3},{5,4},{6,5},{7,6},{4,7},{9,8},{10,9},{11,1... | collective-permute-start | bytes 9224 | tf_op jit(solution)/shard_map/ppermute | solution.py:10
  43.0 7.0 %collective-permute-start.4 = (f32[6,4,32]{0,2,1:T(8,128)S(1)}, f32[6,4,32]{0,2,1:T(8,128)S(1)}, u32[]{:S(2)}, u32[]{:S(2)}) collective-permute-start(f32[6,4,32]{0,2,1:T(8,128)S(1)} %get-tuple-element.19), channel_id=1, source_target_pairs={{28,0},{0,4},{4,8},{8,12},{12,16},{16,20},{20,24},{24,28},{29,1},{... | collective-permute-start | bytes 9224 | tf_op jit(solution)/shard_map/ppermute | solution.py:10
  43.4 6.6 %collective-permute-start.6 = (f32[6,4,32]{0,2,1:T(8,128)S(1)}, f32[6,4,32]{0,2,1:T(8,128)S(1)}, u32[]{:S(2)}, u32[]{:S(2)}) collective-permute-start(f32[6,4,32]{0,2,1:T(8,128)S(1)} %get-tuple-element.20), channel_id=1, source_target_pairs={{3,0},{0,1},{1,2},{2,3},{7,4},{4,5},{5,6},{6,7},{11,8},{8,9},{9,10... | collective-permute-start | bytes 9224 | tf_op jit(solution)/shard_map/ppermute | solution.py:10
  44.8 6.3 %collective-permute-start.5 = (f32[6,4,32]{0,2,1:T(8,128)S(1)}, f32[6,4,32]{0,2,1:T(8,128)S(1)}, u32[]{:S(2)}, u32[]{:S(2)}) collective-permute-start(f32[6,4,32]{0,2,1:T(8,128)S(1)} %get-tuple-element.21), channel_id=1, source_target_pairs={{4,0},{8,4},{12,8},{16,12},{20,16},{24,20},{28,24},{0,28},{5,1},{9... | collective-permute-start | bytes 9224 | tf_op jit(solution)/shard_map/ppermute | solution.py:10
  49.2 1.9 %collective-permute-start.7 = (f32[6,4,32]{0,2,1:T(8,128)S(1)}, f32[6,4,32]{0,2,1:T(8,128)S(1)}, u32[]{:S(2)}, u32[]{:S(2)}) collective-permute-start(f32[6,4,32]{0,2,1:T(8,128)S(1)} %get-tuple-element.22), channel_id=1, source_target_pairs={{1,0},{2,1},{3,2},{0,3},{5,4},{6,5},{7,6},{4,7},{9,8},{10,9},{11,1... | collective-permute-start | bytes 9224 | tf_op jit(solution)/shard_map/ppermute | solution.py:10
  65.8 7.7 %collective-permute-start.8 = (f32[6,4,32]{0,2,1:T(8,128)S(1)}, f32[6,4,32]{0,2,1:T(8,128)S(1)}, u32[]{:S(2)}, u32[]{:S(2)}) collective-permute-start(f32[6,4,32]{0,2,1:T(8,128)S(1)} %get-tuple-element.15), channel_id=1, source_target_pairs={{28,0},{0,4},{4,8},{8,12},{12,16},{16,20},{20,24},{24,28},{29,1},{... | collective-permute-start | bytes 9224 | tf_op jit(solution)/shard_map/ppermute | solution.py:10
  65.9 7.6 %collective-permute-start.10 = (f32[6,4,32]{0,2,1:T(8,128)S(1)}, f32[6,4,32]{0,2,1:T(8,128)S(1)}, u32[]{:S(2)}, u32[]{:S(2)}) collective-permute-start(f32[6,4,32]{0,2,1:T(8,128)S(1)} %get-tuple-element.16), channel_id=1, source_target_pairs={{3,0},{0,1},{1,2},{2,3},{7,4},{4,5},{5,6},{6,7},{11,8},{8,9},{9,10... | collective-permute-start | bytes 9224 | tf_op jit(solution)/shard_map/ppermute | solution.py:10
  67.6 6.3 %collective-permute-start.9 = (f32[6,4,32]{0,2,1:T(8,128)S(1)}, f32[6,4,32]{0,2,1:T(8,128)S(1)}, u32[]{:S(2)}, u32[]{:S(2)}) collective-permute-start(f32[6,4,32]{0,2,1:T(8,128)S(1)} %get-tuple-element.17), channel_id=1, source_target_pairs={{4,0},{8,4},{12,8},{16,12},{20,16},{24,20},{28,24},{0,28},{5,1},{9... | collective-permute-start | bytes 9224 | tf_op jit(solution)/shard_map/ppermute | solution.py:10
  72.0 2.3 %collective-permute-start.11 = (f32[6,4,32]{0,2,1:T(8,128)S(1)}, f32[6,4,32]{0,2,1:T(8,128)S(1)}, u32[]{:S(2)}, u32[]{:S(2)}) collective-permute-start(f32[6,4,32]{0,2,1:T(8,128)S(1)} %get-tuple-element.18), channel_id=1, source_target_pairs={{1,0},{2,1},{3,2},{0,3},{5,4},{6,5},{7,6},{4,7},{9,8},{10,9},{11,1... | collective-permute-start | bytes 9224 | tf_op jit(solution)/shard_map/ppermute | solution.py:10
  87.4 7.9 %copy-start.3 = (f32[6,6,512]{2,1,0:T(8,128)S(1)}, f32[6,6,512]{2,1,0:T(8,128)}, u32[]{:S(2)}) copy-start(f32[6,6,512]{2,1,0:T(8,128)} %param.11) | copy-start | bytes 221188
  89.1 7.4 %collective-permute-start.12 = (f32[6,4,32]{0,2,1:T(8,128)S(1)}, f32[6,4,32]{0,2,1:T(8,128)S(1)}, u32[]{:S(2)}, u32[]{:S(2)}) collective-permute-start(f32[6,4,32]{0,2,1:T(8,128)S(1)} %get-tuple-element.11), channel_id=1, source_target_pairs={{28,0},{0,4},{4,8},{8,12},{12,16},{16,20},{20,24},{24,28},{29,1},{... | collective-permute-start | bytes 9224 | tf_op jit(solution)/shard_map/ppermute | solution.py:10
  89.1 7.4 %collective-permute-start.14 = (f32[6,4,32]{0,2,1:T(8,128)S(1)}, f32[6,4,32]{0,2,1:T(8,128)S(1)}, u32[]{:S(2)}, u32[]{:S(2)}) collective-permute-start(f32[6,4,32]{0,2,1:T(8,128)S(1)} %get-tuple-element.12), channel_id=1, source_target_pairs={{3,0},{0,1},{1,2},{2,3},{7,4},{4,5},{5,6},{6,7},{11,8},{8,9},{9,10... | collective-permute-start | bytes 9224 | tf_op jit(solution)/shard_map/ppermute | solution.py:10
  90.5 6.3 %collective-permute-start.13 = (f32[6,4,32]{0,2,1:T(8,128)S(1)}, f32[6,4,32]{0,2,1:T(8,128)S(1)}, u32[]{:S(2)}, u32[]{:S(2)}) collective-permute-start(f32[6,4,32]{0,2,1:T(8,128)S(1)} %get-tuple-element.13), channel_id=1, source_target_pairs={{4,0},{8,4},{12,8},{16,12},{20,16},{24,20},{28,24},{0,28},{5,1},{9... | collective-permute-start | bytes 9224 | tf_op jit(solution)/shard_map/ppermute | solution.py:10
  94.9 2.3 %collective-permute-start.15 = (f32[6,4,32]{0,2,1:T(8,128)S(1)}, f32[6,4,32]{0,2,1:T(8,128)S(1)}, u32[]{:S(2)}, u32[]{:S(2)}) collective-permute-start(f32[6,4,32]{0,2,1:T(8,128)S(1)} %get-tuple-element.14), channel_id=1, source_target_pairs={{1,0},{2,1},{3,2},{0,3},{5,4},{6,5},{7,6},{4,7},{9,8},{10,9},{11,1... | collective-permute-start | bytes 9224 | tf_op jit(solution)/shard_map/ppermute | solution.py:10
where the time goes:
time: 112 us; the launch traced here: 111 us
  local copies, waits for them, and re-layouts  62.8 us (56%)
  starting transfers between devices  26.7 us (24%)
  other arithmetic  13.6 us (12%)
  waiting for transfers between devices  6.86 us (6%)
    gather x5, local copies, waits for them, and re-layouts, neighbour_sum(): gathered = jnp.take(extended, neighbours, axis=1)  54.1 us
    ppermute x16, starting transfers between devices, from_behind(): return lax.ppermute(block, axis, route)  26.7 us
    unnamed x13, other arithmetic  8.74 us
    ppermute x16, waiting for transfers between devices, from_behind(): return lax.ppermute(block, axis, route)  6.86 us
    gather x4, local copies, waits for them, and re-layouts, shards(): halo_buffer = trade(correction[:, send_lists])  4.14 us
    unnamed x15, local copies, waits for them, and re-layouts  3.76 us
  transfers between devices with their start and end apart: 16, of which 11 were waited for; matrix products, arithmetic and copies ran while one was open for 1% of the time, Pallas kernels for 0%

commit v1 on v0

v1 whole, which is shorter than its diff:
```python
import functools

import jax
import jax.numpy as jnp
from jax import lax
from jax.experimental import pallas as pl
from jax.experimental.pallas import tpu as pltpu
from jax.sharding import PartitionSpec as P

MESH = pl.DeviceIdType.MESH
COLOURS = 4
ROWS = 8
LANES = 128


def take(x, lane):
    return jnp.take_along_axis(x, lane, axis=1, mode="promise_in_bounds")


def spread(row):
    return jnp.broadcast_to(row, (ROWS, LANES))


def padded(x):
    return jnp.concatenate([x, jnp.zeros((ROWS - x.shape[0], LANES), x.dtype)], axis=0)


def row_sums(parts):
    row = lax.broadcasted_iota(jnp.int32, (ROWS, LANES), 0)
    first = []
    for j in range(2):
        x, y = parts[j], parts[j + 4]
        low = row < 4
        first.append(jnp.where(low, x, y) + pltpu.roll(jnp.where(low, y, x), 4, 0))
    for j in range(2, 4):
        x = parts[j]
        first.append(jnp.where(row < 4, x + pltpu.roll(x, 4, 0), 0.0))
    second = []
    for j in range(2):
        x, y = first[j], first[j + 2]
        second.append(jnp.where((row & 2) == 0, x + pltpu.roll(x, 6, 0), y + pltpu.roll(y, 2, 0)))
    x, y = second
    return jnp.where((row & 1) == 0, x + pltpu.roll(x, 7, 0), y + pltpu.roll(y, 1, 0))


def total(terms):
    while len(terms) > 1:
        terms = [sum(terms[i:i + 2][1:], terms[i]) for i in range(0, len(terms), 2)]
    return terms[0]


def kernel(
    n_dom, n_sub,
    rhs_hbm, pre_hbm, diag_hbm, off_hbm, nbr_hbm, send_hbm,
    corr_out, res_out,
    rhs, pre, diag, off, nbr, send_lists,
    off_p, pre_p, lane_of, code_of, outgoing, arrived,
    in_sem, send_sem, recv_sem,
):
    width = rhs.shape[0]
    nbrs = nbr.shape[0]
    blocks = rhs.shape[1] // LANES
    slots = send_lists.shape[2]

    loads = [
        pltpu.make_async_copy(src, dst, in_sem.at[i])
        for i, (src, dst) in enumerate([
            (send_hbm, send_lists), (rhs_hbm, rhs), (pre_hbm, pre),
            (nbr_hbm, nbr), (off_hbm, off), (diag_hbm, diag)])
    ]
    for load in loads:
        load.start()

    i, j = lax.axis_index("dom"), lax.axis_index("sub")
    targets = [
        (lax.rem(i + 1, n_dom), j), (lax.rem(i + n_dom - 1, n_dom), j),
        (i, lax.rem(j + 1, n_sub)), (i, lax.rem(j + n_sub - 1, n_sub)),
    ]
    barrier = pltpu.get_barrier_semaphore()
    for target in targets:
        pl.semaphore_signal(barrier, inc=1, device_id=target, device_id_type=MESH)

    lane = lax.broadcasted_iota(jnp.int32, (ROWS, LANES), 1)
    segment = lane // slots

    loads[0].wait()
    order = jnp.concatenate([send_lists[d] for d in range(4)], axis=1)
    order = padded(order)
    perm = [spread(order[c:c + 1]) for c in range(COLOURS)]

    def permuted(piece, c):
        got = take(padded(piece(0)), perm[c] & 127)
        for s in range(1, blocks):
            got = jnp.where((perm[c] >> 7) == s, take(padded(piece(s)), perm[c] & 127), got)
        return got

    def cut(s):
        return slice(s * LANES, (s + 1) * LANES)

    loads[1].wait()
    rhs_p = [permuted(lambda s: rhs[:, cut(s)], c) for c in range(COLOURS)]
    loads[2].wait()

    def permute_pre(c):
        for a in range(width):
            pre_p[c, a] = permuted(lambda s: pre[a, :, cut(s)], c)

    def apply_pre(c, field):
        return row_sums([pre_p[c, a] * field for a in range(width)])

    permute_pre(0)
    correction = [apply_pre(0, rhs_p[0])]
    outgoing[0] = correction[0]

    pl.semaphore_wait(barrier, 4)

    def copies(c):
        return [
            pltpu.make_async_remote_copy(
                src_ref=outgoing.at[c], dst_ref=arrived.at[c, d],
                send_sem=send_sem.at[c, d], recv_sem=recv_sem.at[c, d],
                device_id=targets[d], device_id_type=MESH)
            for d in range(4)
        ]

    flying = [copies(0)]
    for copy in flying[0]:
        copy.start()

    columns = order.T
    node = lax.broadcasted_iota(jnp.int32, (LANES, LANES), 1)
    lane_down = lax.broadcasted_iota(jnp.int32, (LANES, LANES), 0)
    place = []
    for s in range(blocks):
        hits = jnp.zeros((LANES, LANES), jnp.int32)
        for c in range(COLOURS):
            column = jnp.broadcast_to(columns[:, c:c + 1], (LANES, LANES))
            hits = jnp.where(column == node + s * LANES, lane_down + c * LANES, hits)
        place.append(spread(jnp.sum(hits, axis=0, keepdims=True)))

    loads[3].wait()
    for c in range(COLOURS):
        index = permuted(lambda s: nbr[:, cut(s)], c)
        local = take(place[0], index & 127)
        for s in range(1, blocks):
            local = jnp.where((index >> 7) == s, take(place[s], index & 127), local)
        outside = index >= LANES * blocks
        spot = index - LANES * blocks
        halo_lane = ((spot >> 7) & 3) * slots + (spot & (slots - 1))
        halo_code = 2 * ((spot >> 5) & 3) + 1
        lane_of[c] = jnp.where(outside, halo_lane, local & 127)
        code_of[c] = jnp.where(outside, halo_code, 2 * (local >> 7))

    loads[4].wait()
    live = lax.broadcasted_iota(jnp.int32, (ROWS, LANES), 0) < width

    def permute_off(c):
        def step(k, carry):
            for a in range(width):
                off_p[c, k, a] = permuted(lambda s: off[k, a, :, cut(s)], c)
            return carry
        lax.fori_loop(0, nbrs, step, 0)

    def contribution(c, sources):
        parts = [[] for _ in range(width)]
        for k in range(nbrs):
            where = spread(lane_of[c, k:k + 1])
            code = spread(code_of[c, k:k + 1])
            got = jnp.zeros((ROWS, LANES), jnp.float32)
            for number, block in sources:
                got = jnp.where(code == number, take(block, where), got)
            for a in range(width):
                parts[a].append(off_p[c, k, a] * got)
        return row_sums([total(part) for part in parts])

    halo = []

    def arrive(c):
        for copy in flying[c]:
            copy.wait_recv()
        got = arrived[c, 0]
        for d in range(1, 4):
            got = jnp.where(segment == d, arrived[c, d], got)
        halo.append(got)

    coupled = [jnp.zeros((ROWS, LANES), jnp.float32) for _ in range(COLOURS)]
    for c in range(1, COLOURS):
        permute_pre(c)
        permute_off(c)
        sources = [(2 * e, correction[e]) for e in range(c)]
        sources += [(2 * e + 1, halo[e]) for e in range(c - 1)]
        coupled[c] = contribution(c, sources)
        arrive(c - 1)
        coupled[c] += contribution(c, [(2 * c - 1, halo[c - 1])])
        correction.append(apply_pre(c, rhs_p[c] - coupled[c]))
        outgoing[c] = correction[c]
        flying.append(copies(c))
        for copy in flying[c]:
            copy.start()

    last = COLOURS - 1
    permute_off(0)
    for c in range(COLOURS):
        sources = [(2 * e, correction[e]) for e in range(c, COLOURS)]
        sources += [(2 * e + 1, halo[e]) for e in range(c, last)]
        coupled[c] += contribution(c, sources)

    def natural(fields, s):
        got = take(fields[0], place[s] & 127)
        for c in range(1, COLOURS):
            got = jnp.where((place[s] >> 7) == c, take(fields[c], place[s] & 127), got)
        return got

    loads[5].wait()
    base = []
    for s in range(blocks):
        field = natural(correction, s)
        corr_out[:, cut(s)] = field[:width]
        parts = [padded(diag[a, :, cut(s)]) * field for a in range(width)]
        base.append(padded(rhs[:, cut(s)]) - row_sums(parts))

    arrive(last)
    for c in range(COLOURS):
        coupled[c] += contribution(c, [(2 * last + 1, halo[last])])
    for s in range(blocks):
        res_out[:, cut(s)] = (base[s] - natural(coupled, s))[:width]

    for c in range(COLOURS):
        for copy in flying[c]:
            copy.wait_send()


def shards(n_dom, n_sub, rhs, precond, diag_blocks, off_blocks, neighbours, colours, send_lists):
    width, nodes = rhs.shape
    nbrs = neighbours.shape[0]
    blocks = nodes // LANES
    f32 = jnp.float32
    result = jax.ShapeDtypeStruct((width, nodes), f32)
    return pl.pallas_call(
        functools.partial(kernel, n_dom, n_sub),
        out_shape=(result, result),
        in_specs=[pl.BlockSpec(memory_space=pl.ANY)] * 6,
        out_specs=(pl.BlockSpec(memory_space=pltpu.VMEM),) * 2,
        scratch_shapes=[
            pltpu.VMEM(rhs.shape, f32),
            pltpu.VMEM(precond.shape, f32),
            pltpu.VMEM(diag_blocks.shape, f32),
            pltpu.VMEM(off_blocks.shape, f32),
            pltpu.VMEM(neighbours.shape, jnp.int32),
            pltpu.VMEM(send_lists.shape, jnp.int32),
            pltpu.VMEM((COLOURS, nbrs, width, ROWS, LANES), f32),
            pltpu.VMEM((COLOURS, width, ROWS, LANES), f32),
            pltpu.VMEM((COLOURS, ROWS, LANES), jnp.int32),
            pltpu.VMEM((COLOURS, ROWS, LANES), jnp.int32),
            pltpu.VMEM((COLOURS, ROWS, LANES), f32),
            pltpu.VMEM((COLOURS, 4, ROWS, LANES), f32),
            pltpu.SemaphoreType.DMA((6,)),
            pltpu.SemaphoreType.DMA((COLOURS, 4)),
            pltpu.SemaphoreType.DMA((COLOURS, 4)),
        ],
        compiler_params=pltpu.CompilerParams(
            collective_id=0, has_side_effects=True, vmem_limit_bytes=16 * 2**20),
    )(rhs, precond, diag_blocks, off_blocks, neighbours, send_lists)


def solution(mesh):
    both = ("dom", "sub")
    placed = (
        P(None, both),
        P(None, None, both),
        P(None, None, both),
        P(None, None, None, both),
        P(None, both),
        P(both),
        P(None, None, both),
    )
    return jax.shard_map(
        functools.partial(shards, mesh.shape["dom"], mesh.shape["sub"]),
        mesh=mesh,
        in_specs=placed,
        out_specs=(P(None, both), P(None, both)),
        check_vma=False,
    )
```

time: 112 us -> 30.5 us (0.27)
  local copies, waits for them, and re-layouts: 62.8 us -> 6.18 us
  starting transfers between devices: 26.7 us -> 0 us
  Pallas kernels: 0 us -> 23.3 us
  other arithmetic: 13.6 us -> 0 us
  waiting for transfers between devices: 6.86 us -> 0 us
    gather x9 -> x0, local copies, waits for them, and re-layouts: 58.3 us -> none  [the longest x5 54.1 us: neighbour_sum(): gathered = jnp.take(extended, neighbours, axis=1)]
    ppermute x16 -> x0, starting transfers between devices: 26.7 us -> none  [from_behind(): return lax.ppermute(block, axis, route)]
    pallas_call x0 -> x1, Pallas kernels: none -> 23.3 us  [shards(): pl.pallas_call(functools.partial(kernel, n_dom, n_sub), out_shape=(result...]
    unnamed x13 -> x0, other arithmetic: 8.74 us -> none
    ppermute x16 -> x0, waiting for transfers between devices: 6.86 us -> none  [from_behind(): return lax.ppermute(block, axis, route)]
    unnamed x15 -> x14, local copies, waits for them, and re-layouts: 3.76 us -> 6.18 us
    select_n x6 -> x0, other arithmetic: 2.04 us -> none  [the longest x1 0.72 us: neighbour_sum(): gathered = jnp.take(extended, neighbours, axis=1)]
  transfers between devices with their start and end apart: 16 -> 0, of which waited for: 11 -> 0; matrix products, arithmetic and copies ran while one was open for 1% -> 0% of each run, Pallas kernels for 0% -> 0%
where the time goes in v1:
time: 30.5 us; the launch traced here: 30.1 us
  Pallas kernels  23.3 us (76%)
  local copies, waits for them, and re-layouts  6.18 us (20%)
  between operations  0.65 us (2%)
    pallas_call x1, Pallas kernels, shards(): pl.pallas_call(functools.partial(kernel, n_dom, n_sub), out_shape=(result...  23.3 us
    unnamed x14, local copies, waits for them, and re-layouts  6.18 us

profile of v1, /device:TPU:0, one launch (start us, length us, event | category | flops | bytes accessed | tf_op | source)
XLA Modules:
  0.0 30.1 jit_solution(13708971083884452729)
XLA Ops:
  0.6 0.0 copy-start
  0.6 1.1 %copy-done = f32[6,6,6,512]{3,2,1,0:T(8,128)S(1)} copy-done((f32[6,6,6,512]{3,2,1,0:T(8,128)S(1)}, f32[6,6,6,512]{3,2,1,0:T(8,128)}, u32[]{:S(2)}) %copy-start) | copy-done | bytes 442392
  1.7 0.0 copy-start.1
  1.7 0.9 %copy-done.1 = f32[6,6,512]{2,1,0:T(8,128)S(1)} copy-done((f32[6,6,512]{2,1,0:T(8,128)S(1)}, f32[6,6,512]{2,1,0:T(8,128)}, u32[]{:S(2)}) %copy-start.1) | copy-done | bytes 73752
  2.6 0.0 copy-start.2
  2.6 0.9 %copy-done.2 = f32[6,6,512]{2,1,0:T(8,128)S(1)} copy-done((f32[6,6,512]{2,1,0:T(8,128)S(1)}, f32[6,6,512]{2,1,0:T(8,128)}, u32[]{:S(2)}) %copy-start.2) | copy-done | bytes 73752
  3.5 0.0 copy-start.3
  3.5 0.7 %copy-done.3 = f32[6,512]{1,0:T(8,128)S(1)} copy-done((f32[6,512]{1,0:T(8,128)S(1)}, f32[6,512]{1,0:T(8,128)}, u32[]{:S(2)}) %copy-start.3) | copy-done | bytes 12312
  4.2 0.0 copy-start.4
  4.2 0.7 %copy-done.4 = s32[6,512]{1,0:T(8,128)S(1)} copy-done((s32[6,512]{1,0:T(8,128)S(1)}, s32[6,512]{1,0:T(8,128)}, u32[]{:S(2)}) %copy-start.4) | copy-done | bytes 12312
  4.9 0.0 copy-start.5
  4.9 0.7 %copy-done.5 = s32[4,4,32]{2,1,0:T(4,128)S(1)} copy-done((s32[4,4,32]{2,1,0:T(4,128)S(1)}, s32[4,4,32]{2,1,0:T(4,128)}, u32[]{:S(2)}) %copy-start.5) | copy-done | bytes 2072
  5.6 23.3 %shard_map.77 = (f32[6,512]{1,0:T(8,128)S(1)}, f32[6,512]{1,0:T(8,128)S(1)}) custom-call(f32[6,512]{1,0:T(8,128)S(1)} %copy-done.3, f32[6,6,512]{2,1,0:T(8,128)S(1)} %copy-done.1, f32[6,6,512]{2,1,0:T(8,128)S(1)} %copy-done.2, f32[6,6,6,512]{3,2,1,0:T(8,128)S(1)} %copy-done, s32[6,512]{1,0:T(8,128)S(1)} %copy-done.4, s32[4,4,32]{2,1,0:T(4,128)S(1)} %copy-done.5), custom_call_target="tpu_custom_call" | custom-call | tf_op jit(solution)/shard_map/pallas_call | solution.py:239
  28.9 0.6 %copy.10 = f32[6,512]{1,0:T(8,128)} copy(f32[6,512]{1,0:T(8,128)S(1)} %get-tuple-element.4) | data formatting | bytes 24576
  29.5 0.6 %copy.11 = f32[6,512]{1,0:T(8,128)} copy(f32[6,512]{1,0:T(8,128)S(1)} %get-tuple-element.5) | data formatting | bytes 24576
Async XLA Ops:
  0.6 1.1 %copy-start = (f32[6,6,6,512]{3,2,1,0:T(8,128)S(1)}, f32[6,6,6,512]{3,2,1,0:T(8,128)}, u32[]{:S(2)}) copy-start(f32[6,6,6,512]{3,2,1,0:T(8,128)} %off_hbm.1) | copy-start | bytes 1327108
  1.7 0.9 %copy-start.1 = (f32[6,6,512]{2,1,0:T(8,128)S(1)}, f32[6,6,512]{2,1,0:T(8,128)}, u32[]{:S(2)}) copy-start(f32[6,6,512]{2,1,0:T(8,128)} %pre_hbm.1) | copy-start | bytes 221188
  2.6 0.9 %copy-start.2 = (f32[6,6,512]{2,1,0:T(8,128)S(1)}, f32[6,6,512]{2,1,0:T(8,128)}, u32[]{:S(2)}) copy-start(f32[6,6,512]{2,1,0:T(8,128)} %diag_hbm.1) | copy-start | bytes 221188
  3.5 0.7 %copy-start.3 = (f32[6,512]{1,0:T(8,128)S(1)}, f32[6,512]{1,0:T(8,128)}, u32[]{:S(2)}) copy-start(f32[6,512]{1,0:T(8,128)} %rhs_hbm.1) | copy-start | bytes 36868
  4.2 0.7 %copy-start.4 = (s32[6,512]{1,0:T(8,128)S(1)}, s32[6,512]{1,0:T(8,128)}, u32[]{:S(2)}) copy-start(s32[6,512]{1,0:T(8,128)} %nbr_hbm.1) | copy-start | bytes 36868
  4.9 0.7 %copy-start.5 = (s32[4,4,32]{2,1,0:T(4,128)S(1)}, s32[4,4,32]{2,1,0:T(4,128)}, u32[]{:S(2)}) copy-start(s32[4,4,32]{2,1,0:T(4,128)} %send_hbm.1) | copy-start | bytes 6148

commit v2 on v1

--- a/solution.py
+++ b/solution.py
@@ -52,11 +52,12 @@
 def kernel(
     n_dom, n_sub,
     rhs_hbm, pre_hbm, diag_hbm, off_hbm, nbr_hbm, send_hbm,
-    corr_out, res_out,
+    both_out,
     rhs, pre, diag, off, nbr, send_lists,
     off_p, pre_p, lane_of, code_of, outgoing, arrived,
     in_sem, send_sem, recv_sem,
 ):
+    corr_out, res_out = both_out.at[0], both_out.at[1]
     width = rhs.shape[0]
     nbrs = nbr.shape[0]
     blocks = rhs.shape[1] // LANES
@@ -233,14 +234,13 @@
 def shards(n_dom, n_sub, rhs, precond, diag_blocks, off_blocks, neighbours, colours, send_lists):
     width, nodes = rhs.shape
     nbrs = neighbours.shape[0]
-    blocks = nodes // LANES
     f32 = jnp.float32
-    result = jax.ShapeDtypeStruct((width, nodes), f32)
-    return pl.pallas_call(
+    arrays = (rhs, precond, diag_blocks, off_blocks, neighbours, send_lists)
+    both = pl.pallas_call(
         functools.partial(kernel, n_dom, n_sub),
-        out_shape=(result, result),
-        in_specs=[pl.BlockSpec(memory_space=pl.ANY)] * 6,
-        out_specs=(pl.BlockSpec(memory_space=pltpu.VMEM),) * 2,
+        out_shape=jax.ShapeDtypeStruct((2, width, nodes), f32),
+        in_specs=[pl.BlockSpec(memory_space=pltpu.HBM)] * 6,
+        out_specs=pl.BlockSpec(memory_space=pltpu.VMEM),
         scratch_shapes=[
             pltpu.VMEM(rhs.shape, f32),
             pltpu.VMEM(precond.shape, f32),
@@ -260,7 +260,8 @@
         ],
         compiler_params=pltpu.CompilerParams(
             collective_id=0, has_side_effects=True, vmem_limit_bytes=16 * 2**20),
-    )(rhs, precond, diag_blocks, off_blocks, neighbours, send_lists)
+    )(*[pltpu.with_memory_space_constraint(x, pltpu.HBM) for x in arrays])
+    return both[0], both[1]
 
 
 def solution(mesh):

time: 30.5 us -> 24.3 us (0.80)
  local copies, waits for them, and re-layouts: 6.18 us -> 0.62 us
  Pallas kernels: 23.3 us -> 22.9 us
    unnamed x14 -> x0, local copies, waits for them, and re-layouts: 6.18 us -> none
    squeeze x0 -> x1, local copies, waits for them, and re-layouts: none -> 0.62 us  [shards(): return (both[0], both[1])]
    pallas_call x1, Pallas kernels: 23.3 us -> 22.9 us  [shards(): pl.pallas_call(functools.partial(kernel, n_dom, n_sub), out_shape=jax.Sha...]
where the time goes in v2:
time: 24.3 us; the launch traced here: 24.1 us
  Pallas kernels  22.9 us (94%)
  between operations  0.64 us (3%)
  local copies, waits for them, and re-layouts  0.62 us (3%)
    pallas_call x1, Pallas kernels, shards(): pl.pallas_call(functools.partial(kernel, n_dom, n_sub), out_shape=jax.Sha...  22.9 us
    squeeze x1, local copies, waits for them, and re-layouts, shards(): return (both[0], both[1])  0.62 us

profile of v2, /device:TPU:0, one launch (start us, length us, event | category | flops | bytes accessed | tf_op | source)
XLA Modules:
  0.0 24.1 jit_solution(7507335122818745116)
XLA Ops:
  0.6 22.9 %shard_map.77 = f32[2,6,512]{2,1,0:T(8,128)S(1)} custom-call(f32[6,512]{1,0:T(8,128)} %rhs_hbm.1, f32[6,6,512]{2,1,0:T(8,128)} %pre_hbm.1, f32[6,6,512]{2,1,0:T(8,128)} %diag_hbm.1, f32[6,6,6,512]{3,2,1,0:T(8,128)} %off_hbm.1, s32[6,512]{1,0:T(8,128)} %nbr_hbm.1, s32[4,4,32]{2,1,0:T(4,128)} %send_hbm.1), custom_call_target="tpu_custom_call" | custom-call | tf_op jit(solution)/shard_map/pallas_call | solution.py:239
  23.5 0.6 %slice_bitcast_fusion = (f32[6,512]{1,0:T(8,128)}, f32[6,512]{1,0:T(8,128)}) fusion(f32[2,6,512]{2,1,0:T(8,128)S(1)} %shard_map.77), kind=kLoop, calls=%fused_computation | loop fusion | bytes 49152 | tf_op jit(solution)/shard_map/squeeze | solution.py:264

commit v3 on v2

--- a/solution.py
+++ b/solution.py
@@ -55,13 +55,15 @@
     both_out,
     rhs, pre, diag, off, nbr, send_lists,
     off_p, pre_p, lane_of, code_of, outgoing, arrived,
-    in_sem, send_sem, recv_sem,
+    kit, kit_in, spots, spots_in, rest, rest_in,
+    in_sem, send_sem, recv_sem, kit_send_sem, kit_recv_sem,
 ):
     corr_out, res_out = both_out.at[0], both_out.at[1]
     width = rhs.shape[0]
     nbrs = nbr.shape[0]
     blocks = rhs.shape[1] // LANES
     slots = send_lists.shape[2]
+    groups = pl.cdiv(nbrs, 4)
 
     loads = [
         pltpu.make_async_copy(src, dst, in_sem.at[i])
@@ -115,18 +117,25 @@
 
     pl.semaphore_wait(barrier, 4)
 
-    def copies(c):
-        return [
-            pltpu.make_async_remote_copy(
+    def send(c, directions):
+        started = {
+            d: pltpu.make_async_remote_copy(
                 src_ref=outgoing.at[c], dst_ref=arrived.at[c, d],
                 send_sem=send_sem.at[c, d], recv_sem=recv_sem.at[c, d],
                 device_id=targets[d], device_id_type=MESH)
-            for d in range(4)
-        ]
-
-    flying = [copies(0)]
-    for copy in flying[0]:
-        copy.start()
+            for d in directions
+        }
+        for copy in started.values():
+            copy.start()
+        return started
+
+    flying = [send(0, range(4))]
+    kit_copies = [
+        pltpu.make_async_remote_copy(
+            src_ref=src, dst_ref=dst, send_sem=kit_send_sem.at[n], recv_sem=kit_recv_sem.at[n],
+            device_id=targets[0], device_id_type=MESH)
+        for n, (src, dst) in enumerate([(kit, kit_in), (spots, spots_in), (rest, rest_in)])
+    ]
 
     columns = order.T
     node = lax.broadcasted_iota(jnp.int32, (LANES, LANES), 1)
@@ -176,13 +185,50 @@
 
     halo = []
 
-    def arrive(c):
-        for copy in flying[c]:
+    def arrive(c, got=None):
+        for copy in flying[c].values():
             copy.wait_recv()
-        got = arrived[c, 0]
-        for d in range(1, 4):
-            got = jnp.where(segment == d, arrived[c, d], got)
+        for d in flying[c]:
+            got = arrived[c, d] if got is None else jnp.where(segment == d, arrived[c, d], got)
         halo.append(got)
+
+    def send_kit():
+        mine = (code_of[1] == 1) & (lane_of[1] // slots == 1)
+        reads = jnp.where(mine, lane_of[1], -1)
+        for g in range(groups):
+            spot = jnp.full((ROWS, LANES), -1, jnp.int32)
+            for q in range(min(4, nbrs - 4 * g)):
+                k = 4 * g + q
+                moved = pltpu.roll(spread(reads[k:k + 1]), q * slots, 1)
+                spot = jnp.where(segment == q, moved, spot)
+            spots[g] = spot
+        for a in range(width):
+            for g in range(groups):
+                tile = jnp.zeros((ROWS, LANES), jnp.float32)
+                for q in range(min(4, nbrs - 4 * g)):
+                    moved = pltpu.roll(off_p[1, 4 * g + q, a], q * slots, 1)
+                    tile = jnp.where(segment == q, moved, tile)
+                kit[a * groups + g] = tile
+            kit[width * groups + a] = pre_p[1, a]
+        kit_copies[0].start()
+        kit_copies[1].start()
+
+    def from_kit():
+        kit_copies[0].wait_recv()
+        kit_copies[1].wait_recv()
+        reads = []
+        for g in range(groups):
+            spot = spots_in[g]
+            reads.append(jnp.where(spot >= 0, take(correction[0], spot & 127), 0.0))
+        parts = [
+            total([kit_in[a * groups + g] * reads[g] for g in range(groups)]) for a in range(width)
+        ]
+        coupling = row_sums(parts)
+        coupling += pltpu.roll(coupling, 2 * slots, 1)
+        coupling += pltpu.roll(coupling, slots, 1)
+        kit_copies[2].wait_recv()
+        field = rest_in[...] - coupling
+        return row_sums([kit_in[width * groups + a] * field for a in range(width)])
 
     coupled = [jnp.zeros((ROWS, LANES), jnp.float32) for _ in range(COLOURS)]
     for c in range(1, COLOURS):
@@ -191,13 +237,25 @@
         sources = [(2 * e, correction[e]) for e in range(c)]
         sources += [(2 * e + 1, halo[e]) for e in range(c - 1)]
         coupled[c] = contribution(c, sources)
-        arrive(c - 1)
-        coupled[c] += contribution(c, [(2 * c - 1, halo[c - 1])])
+        if c == 1:
+            send_kit()
+            others = jnp.zeros((ROWS, LANES), jnp.float32)
+            for d in (2, 3, 0):
+                flying[0][d].wait_recv()
+                others = jnp.where(segment == d, arrived[0, d], others)
+            coupled[1] += contribution(1, [(1, others)])
+            rest[...] = rhs_p[1] - coupled[1]
+            kit_copies[2].start()
+            flying[0][1].wait_recv()
+            upper = jnp.where(segment == 1, arrived[0, 1], 0.0)
+            halo.append(others + upper)
+            coupled[1] += contribution(1, [(1, upper)])
+        else:
+            arrive(c - 1, from_kit() if c == 2 else None)
+            coupled[c] += contribution(c, [(2 * c - 1, halo[c - 1])])
         correction.append(apply_pre(c, rhs_p[c] - coupled[c]))
         outgoing[c] = correction[c]
-        flying.append(copies(c))
-        for copy in flying[c]:
-            copy.start()
+        flying.append(send(c, range(1, 4) if c == 1 else range(4)))
 
     last = COLOURS - 1
     permute_off(0)
@@ -227,14 +285,18 @@
         res_out[:, cut(s)] = (base[s] - natural(coupled, s))[:width]
 
     for c in range(COLOURS):
-        for copy in flying[c]:
+        for copy in flying[c].values():
             copy.wait_send()
+    for copy in kit_copies:
+        copy.wait_send()
 
 
 def shards(n_dom, n_sub, rhs, precond, diag_blocks, off_blocks, neighbours, colours, send_lists):
     width, nodes = rhs.shape
     nbrs = neighbours.shape[0]
     f32 = jnp.float32
+    groups = pl.cdiv(nbrs, 4)
+    tiles = width * groups + width
     arrays = (rhs, precond, diag_blocks, off_blocks, neighbours, send_lists)
     both = pl.pallas_call(
         functools.partial(kernel, n_dom, n_sub),
@@ -254,9 +316,14 @@
             pltpu.VMEM((COLOURS, ROWS, LANES), jnp.int32),
             pltpu.VMEM((COLOURS, ROWS, LANES), f32),
             pltpu.VMEM((COLOURS, 4, ROWS, LANES), f32),
+            *[pltpu.VMEM((tiles, ROWS, LANES), f32)] * 2,
+            *[pltpu.VMEM((groups, ROWS, LANES), jnp.int32)] * 2,
+            *[pltpu.VMEM((ROWS, LANES), f32)] * 2,
             pltpu.SemaphoreType.DMA((6,)),
             pltpu.SemaphoreType.DMA((COLOURS, 4)),
             pltpu.SemaphoreType.DMA((COLOURS, 4)),
+            pltpu.SemaphoreType.DMA((3,)),
+            pltpu.SemaphoreType.DMA((3,)),
         ],
         compiler_params=pltpu.CompilerParams(
             collective_id=0, has_side_effects=True, vmem_limit_bytes=16 * 2**20),

time: 24.3 us -> 21.9 us (0.901)
  Pallas kernels: 22.9 us -> 20.5 us
    pallas_call x1, Pallas kernels: 22.9 us -> 20.5 us  [shards(): pl.pallas_call(functools.partial(kernel, n_dom, n_sub), out_shape=jax.Sha...]
where the time goes in v3:
time: 21.9 us; the launch traced here: 21.7 us
  Pallas kernels  20.5 us (94%)
  between operations  0.64 us (3%)
  local copies, waits for them, and re-layouts  0.62 us (3%)
    pallas_call x1, Pallas kernels, shards(): pl.pallas_call(functools.partial(kernel, n_dom, n_sub), out_shape=jax.Sha...  20.5 us
    squeeze x1, local copies, waits for them, and re-layouts, shards(): return (both[0], both[1])  0.62 us

profile of v3, /device:TPU:0, one launch (start us, length us, event | category | flops | bytes accessed | tf_op | source)
XLA Modules:
  0.0 21.7 jit_solution(9263424507648665099)
XLA Ops:
  0.6 20.5 %shard_map.77 = f32[2,6,512]{2,1,0:T(8,128)S(1)} custom-call(f32[6,512]{1,0:T(8,128)} %rhs_hbm.1, f32[6,6,512]{2,1,0:T(8,128)} %pre_hbm.1, f32[6,6,512]{2,1,0:T(8,128)} %diag_hbm.1, f32[6,6,6,512]{3,2,1,0:T(8,128)} %off_hbm.1, s32[6,512]{1,0:T(8,128)} %nbr_hbm.1, s32[4,4,32]{2,1,0:T(4,128)} %send_hbm.1), custom_call_target="tpu_custom_call" | custom-call | tf_op jit(solution)/shard_map/pallas_call | solution.py:301
  21.1 0.6 %slice_bitcast_fusion = (f32[6,512]{1,0:T(8,128)}, f32[6,512]{1,0:T(8,128)}) fusion(f32[2,6,512]{2,1,0:T(8,128)S(1)} %shard_map.77), kind=kLoop, calls=%fused_computation | loop fusion | bytes 49152 | tf_op jit(solution)/shard_map/squeeze | solution.py:331

commit v4 on v3

--- a/solution.py
+++ b/solution.py
@@ -11,6 +11,7 @@
 COLOURS = 4
 ROWS = 8
 LANES = 128
+KITS = {1: 0, 3: 1}
 
 
 def take(x, lane):
@@ -101,7 +102,7 @@
         return slice(s * LANES, (s + 1) * LANES)
 
     loads[1].wait()
-    rhs_p = [permuted(lambda s: rhs[:, cut(s)], c) for c in range(COLOURS)]
+    rhs_p = [permuted(lambda s: rhs[:, cut(s)], 0)]
     loads[2].wait()
 
     def permute_pre(c):
@@ -130,12 +131,18 @@
         return started
 
     flying = [send(0, range(4))]
-    kit_copies = [
-        pltpu.make_async_remote_copy(
-            src_ref=src, dst_ref=dst, send_sem=kit_send_sem.at[n], recv_sem=kit_recv_sem.at[n],
-            device_id=targets[0], device_id_type=MESH)
-        for n, (src, dst) in enumerate([(kit, kit_in), (spots, spots_in), (rest, rest_in)])
-    ]
+    kit_copies = {
+        c: [
+            pltpu.make_async_remote_copy(
+                src_ref=src.at[d], dst_ref=dst.at[d],
+                send_sem=kit_send_sem.at[d, n], recv_sem=kit_recv_sem.at[d, n],
+                device_id=targets[d], device_id_type=MESH)
+            for n, (src, dst) in enumerate([(kit, kit_in), (spots, spots_in), (rest, rest_in)])
+        ]
+        for c, d in KITS.items()
+    }
+
+    rhs_p += [permuted(lambda s: rhs[:, cut(s)], c) for c in range(1, COLOURS)]
 
     columns = order.T
     node = lax.broadcasted_iota(jnp.int32, (LANES, LANES), 1)
@@ -192,43 +199,48 @@
             got = arrived[c, d] if got is None else jnp.where(segment == d, arrived[c, d], got)
         halo.append(got)
 
-    def send_kit():
-        mine = (code_of[1] == 1) & (lane_of[1] // slots == 1)
-        reads = jnp.where(mine, lane_of[1], -1)
+    def send_kit(c):
+        d = KITS[c]
+        mine = (code_of[c] == 2 * c - 1) & (lane_of[c] // slots == 1 - d)
+        reads = jnp.where(mine, lane_of[c], -1)
+
+        def moved(x, q):
+            shift = (q - d) % 4 * slots
+            return pltpu.roll(x, shift, 1) if shift else x
+
         for g in range(groups):
             spot = jnp.full((ROWS, LANES), -1, jnp.int32)
             for q in range(min(4, nbrs - 4 * g)):
                 k = 4 * g + q
-                moved = pltpu.roll(spread(reads[k:k + 1]), q * slots, 1)
-                spot = jnp.where(segment == q, moved, spot)
-            spots[g] = spot
+                spot = jnp.where(segment == q, moved(spread(reads[k:k + 1]), q), spot)
+            spots[d, g] = spot
         for a in range(width):
             for g in range(groups):
                 tile = jnp.zeros((ROWS, LANES), jnp.float32)
                 for q in range(min(4, nbrs - 4 * g)):
-                    moved = pltpu.roll(off_p[1, 4 * g + q, a], q * slots, 1)
-                    tile = jnp.where(segment == q, moved, tile)
-                kit[a * groups + g] = tile
-            kit[width * groups + a] = pre_p[1, a]
-        kit_copies[0].start()
-        kit_copies[1].start()
-
-    def from_kit():
-        kit_copies[0].wait_recv()
-        kit_copies[1].wait_recv()
+                    tile = jnp.where(segment == q, moved(off_p[c, 4 * g + q, a], q), tile)
+                kit[d, a * groups + g] = tile
+            kit[d, width * groups + a] = pre_p[c, a]
+        kit_copies[c][0].start()
+        kit_copies[c][1].start()
+
+    def from_kit(c):
+        d = KITS[c]
+        kit_copies[c][0].wait_recv()
+        kit_copies[c][1].wait_recv()
         reads = []
         for g in range(groups):
-            spot = spots_in[g]
-            reads.append(jnp.where(spot >= 0, take(correction[0], spot & 127), 0.0))
+            spot = spots_in[d, g]
+            reads.append(jnp.where(spot >= 0, take(correction[c - 1], spot & 127), 0.0))
         parts = [
-            total([kit_in[a * groups + g] * reads[g] for g in range(groups)]) for a in range(width)
+            total([kit_in[d, a * groups + g] * reads[g] for g in range(groups)]) for a in range(width)
         ]
         coupling = row_sums(parts)
         coupling += pltpu.roll(coupling, 2 * slots, 1)
         coupling += pltpu.roll(coupling, slots, 1)
-        kit_copies[2].wait_recv()
-        field = rest_in[...] - coupling
-        return row_sums([kit_in[width * groups + a] * field for a in range(width)])
+        kit_copies[c][2].wait_recv()
+        field = rest_in[d] - coupling
+        return row_sums([kit_in[d, width * groups + a] * field for a in range(width)])
 
     coupled = [jnp.zeros((ROWS, LANES), jnp.float32) for _ in range(COLOURS)]
     for c in range(1, COLOURS):
@@ -237,25 +249,29 @@
         sources = [(2 * e, correction[e]) for e in range(c)]
         sources += [(2 * e + 1, halo[e]) for e in range(c - 1)]
         coupled[c] = contribution(c, sources)
-        if c == 1:
-            send_kit()
-            others = jnp.zeros((ROWS, LANES), jnp.float32)
-            for d in (2, 3, 0):
-                flying[0][d].wait_recv()
-                others = jnp.where(segment == d, arrived[0, d], others)
-            coupled[1] += contribution(1, [(1, others)])
-            rest[...] = rhs_p[1] - coupled[1]
-            kit_copies[2].start()
-            flying[0][1].wait_recv()
-            upper = jnp.where(segment == 1, arrived[0, 1], 0.0)
-            halo.append(others + upper)
-            coupled[1] += contribution(1, [(1, upper)])
+        known = from_kit(c - 1) if c - 1 in KITS else None
+        if c in KITS:
+            send_kit(c)
+            d = KITS[c]
+            others = jnp.zeros((ROWS, LANES), jnp.float32) if known is None else known
+            for e in flying[c - 1]:
+                if e != 1 - d:
+                    flying[c - 1][e].wait_recv()
+                    others = jnp.where(segment == e, arrived[c - 1, e], others)
+            others = jnp.where(segment == 1 - d, 0.0, others)
+            coupled[c] += contribution(c, [(2 * c - 1, others)])
+            rest[d] = rhs_p[c] - coupled[c]
+            kit_copies[c][2].start()
+            flying[c - 1][1 - d].wait_recv()
+            back = jnp.where(segment == 1 - d, arrived[c - 1, 1 - d], 0.0)
+            halo.append(others + back)
+            coupled[c] += contribution(c, [(2 * c - 1, back)])
         else:
-            arrive(c - 1, from_kit() if c == 2 else None)
+            arrive(c - 1, known)
             coupled[c] += contribution(c, [(2 * c - 1, halo[c - 1])])
         correction.append(apply_pre(c, rhs_p[c] - coupled[c]))
         outgoing[c] = correction[c]
-        flying.append(send(c, range(1, 4) if c == 1 else range(4)))
+        flying.append(send(c, [d for d in range(4) if d != KITS.get(c)]))
 
     last = COLOURS - 1
     permute_off(0)
@@ -278,7 +294,7 @@
         parts = [padded(diag[a, :, cut(s)]) * field for a in range(width)]
         base.append(padded(rhs[:, cut(s)]) - row_sums(parts))
 
-    arrive(last)
+    arrive(last, from_kit(last) if last in KITS else None)
     for c in range(COLOURS):
         coupled[c] += contribution(c, [(2 * last + 1, halo[last])])
     for s in range(blocks):
@@ -287,8 +303,9 @@
     for c in range(COLOURS):
         for copy in flying[c].values():
             copy.wait_send()
-    for copy in kit_copies:
-        copy.wait_send()
+    for started in kit_copies.values():
+        for copy in started:
+            copy.wait_send()
 
 
 def shards(n_dom, n_sub, rhs, precond, diag_blocks, off_blocks, neighbours, colours, send_lists):
@@ -316,14 +333,14 @@
             pltpu.VMEM((COLOURS, ROWS, LANES), jnp.int32),
             pltpu.VMEM((COLOURS, ROWS, LANES), f32),
             pltpu.VMEM((COLOURS, 4, ROWS, LANES), f32),
-            *[pltpu.VMEM((tiles, ROWS, LANES), f32)] * 2,
-            *[pltpu.VMEM((groups, ROWS, LANES), jnp.int32)] * 2,
-            *[pltpu.VMEM((ROWS, LANES), f32)] * 2,
+            *[pltpu.VMEM((2, tiles, ROWS, LANES), f32)] * 2,
+            *[pltpu.VMEM((2, groups, ROWS, LANES), jnp.int32)] * 2,
+            *[pltpu.VMEM((2, ROWS, LANES), f32)] * 2,
             pltpu.SemaphoreType.DMA((6,)),
             pltpu.SemaphoreType.DMA((COLOURS, 4)),
             pltpu.SemaphoreType.DMA((COLOURS, 4)),
-            pltpu.SemaphoreType.DMA((3,)),
-            pltpu.SemaphoreType.DMA((3,)),
+            pltpu.SemaphoreType.DMA((2, 3)),
+            pltpu.SemaphoreType.DMA((2, 3)),
         ],
         compiler_params=pltpu.CompilerParams(
             collective_id=0, has_side_effects=True, vmem_limit_bytes=16 * 2**20),

time: 21.9 us -> 22.2 us (1.014)
    pallas_call x1, Pallas kernels: 20.5 us -> 20.7 us  [shards(): pl.pallas_call(functools.partial(kernel, n_dom, n_sub), out_shape=jax.Sha...]
where the time goes in v4:
time: 22.2 us; the launch traced here: 22 us
  Pallas kernels  20.7 us (93%)
  between operations  0.64 us (3%)
  local copies, waits for them, and re-layouts  0.62 us (3%)
    pallas_call x1, Pallas kernels, shards(): pl.pallas_call(functools.partial(kernel, n_dom, n_sub), out_shape=jax.Sha...  20.7 us
    squeeze x1, local copies, waits for them, and re-layouts, shards(): return (both[0], both[1])  0.62 us

profile of v4, /device:TPU:0, one launch (start us, length us, event | category | flops | bytes accessed | tf_op | source)
XLA Modules:
  0.0 22.0 jit_solution(10665062303248728159)
XLA Ops:
  0.6 20.7 %shard_map.77 = f32[2,6,512]{2,1,0:T(8,128)S(1)} custom-call(f32[6,512]{1,0:T(8,128)} %rhs_hbm.1, f32[6,6,512]{2,1,0:T(8,128)} %pre_hbm.1, f32[6,6,512]{2,1,0:T(8,128)} %diag_hbm.1, f32[6,6,6,512]{3,2,1,0:T(8,128)} %off_hbm.1, s32[6,512]{1,0:T(8,128)} %nbr_hbm.1, s32[4,4,32]{2,1,0:T(4,128)} %send_hbm.1), custom_call_target="tpu_custom_call" | custom-call | tf_op jit(solution)/shard_map/pallas_call | solution.py:318
  21.4 0.6 %slice_bitcast_fusion = (f32[6,512]{1,0:T(8,128)}, f32[6,512]{1,0:T(8,128)}) fusion(f32[2,6,512]{2,1,0:T(8,128)S(1)} %shard_map.77), kind=kLoop, calls=%fused_computation | loop fusion | bytes 49152 | tf_op jit(solution)/shard_map/squeeze | solution.py:348
